TPU v7x, 32 devices: a whole 2x2x4 slice. The times are simulated.
32 devices in a mesh: dp: 1, expert: 32 (over z, y, x, core).
Axes of the slice: x: 2, y: 2, z: 4, core: 2. Of those that a mesh axis runs over, the one named last changes fastest.
Arguments:
- queries: bfloat16 [1024, 4096], P('dp', 'expert'), may hold values from -140 to 140
- keys: bfloat16 [1024, 256], P(('dp', 'expert')), may hold values from -4 to 4
- values: bfloat16 [1024, 256], P(('dp', 'expert')), may hold values from -4 to 4
- span_ids: int32 [1024], P('dp'), may hold values from 0 to 9, as said below
- residual: bfloat16 [1024, 4096], P(('dp', 'expert')), may hold values from -6 to 6
- norm_gain: float32 [4096], replicated, may hold values from 0.1 to 1.9
- routes: int32 [1024, 8], P(('dp', 'expert')), may hold values from 0 to 127, as said below
- gates: float32 [1024, 8], P(('dp', 'expert')), may hold values from 0.2 to 1
- w_gate: bfloat16 [4096, 4096], P('expert'), may hold values from -0.09375 to 0.09375
- w_up: bfloat16 [4096, 4096], P('expert'), may hold values from -0.09375 to 0.09375
- w_down: bfloat16 [4096, 4096], P('expert'), may hold values from -0.1875 to 0.1875
Outputs:
- mixed: bfloat16 [1024, 4096], P(('dp', 'expert'))
Inputs may be any that keep to these rules, and one draw needn't show every extreme that they name: `span_ids`: span numbers start at 0 and never fall along the positions; every span starts at an even position, has 2 to 512 positions and never crosses a multiple of 512; one aligned block of 512 positions is a single span, and every other holds exactly 9 spans. `routes`: each row names 8 different experts. In the rows of one device (aligned blocks of 32 rows) each expert below 4 is named by at most 8 rows, and exactly one such expert, changing from block to block, by exactly 8 rows; every expert below 4 is that one in some block.
All inputs are finite; a program needn't handle non-finite values.
Results may differ from a plain program's by a relative error of at most 0.0054.
Values may be sent and summed in bfloat16 or wider, within the bound.
A program may use at most 64 MiB of HBM per device.

v0:
```python
import math
import jax
import jax.numpy as jnp
from jax import lax
from jax.sharding import PartitionSpec as P

KV_HEADS = 4
HEAD_DIM = 64
FF_WIN = 1024
SPAN = 512


def from_partner(value, axis, distance):
    mask = 2**distance
    pairs = [(source, source ^ mask) for source in range(lax.axis_size(axis))]
    return lax.ppermute(value, axis, pairs)


def attend(queries, key_mine, value_mine, span_ids):
    tokens_all, head_width = queries.shape
    heads_here = head_width // HEAD_DIM
    blocks = tokens_all // SPAN
    score_scale = 1.0 / math.sqrt(HEAD_DIM)
    positions = jnp.arange(SPAN)
    causal = positions[None, :] <= positions[:, None]

    def one_block(pieces):
        query_blk, key_blk, value_blk, ids_blk = pieces
        scores = (
            jnp.einsum("qhd,kd->hqk", query_blk, key_blk, preferred_element_type=jnp.float32)
            * score_scale
        )
        allowed = causal & (ids_blk[None, :] == ids_blk[:, None])
        scores = jnp.where(allowed[None], scores, -jnp.inf)
        highest = jnp.max(scores, axis=-1, keepdims=True)
        raised = jnp.exp(scores - highest)
        attn_weights = (raised / jnp.sum(raised, axis=-1, keepdims=True)).astype(jnp.bfloat16)
        attended_blk = jnp.einsum(
            "hqk,kd->qhd", attn_weights, value_blk, preferred_element_type=jnp.float32
        )
        return attended_blk.astype(jnp.bfloat16)

    result = lax.map(
        one_block,
        (
            queries.reshape(blocks, SPAN, heads_here, HEAD_DIM),
            key_mine.reshape(blocks, SPAN, HEAD_DIM),
            value_mine.reshape(blocks, SPAN, HEAD_DIM),
            span_ids.reshape(blocks, SPAN),
        ),
    )
    return result.reshape(tokens_all, head_width)


def shards(
    queries, keys, values, span_ids, residual, norm_gain, routes, gates, w_gate, w_up, w_down
):
    devices = lax.axis_size("expert")
    my_index = lax.axis_index("expert")
    tok_local = residual.shape[0]
    joined = jnp.concatenate(
        [
            keys.reshape(tok_local, KV_HEADS, HEAD_DIM),
            values.reshape(tok_local, KV_HEADS, HEAD_DIM),
        ],
        axis=2,
    )
    spread = jnp.repeat(joined, devices // KV_HEADS, axis=1)
    arrived_heads = lax.all_to_all(spread, "expert", split_axis=1, concat_axis=0, tiled=True)
    key_mine = arrived_heads[:, 0, :HEAD_DIM]
    value_mine = arrived_heads[:, 0, HEAD_DIM:]
    attended_heads = attend(queries, key_mine, value_mine, span_ids)
    attended = lax.all_to_all(attended_heads, "expert", split_axis=0, concat_axis=1, tiled=True)
    stream_wide = residual.astype(jnp.float32) + attended.astype(jnp.float32)
    stream = stream_wide.astype(jnp.bfloat16)
    stream_wide = stream.astype(jnp.float32)
    inverse = lax.rsqrt(jnp.mean(stream_wide * stream_wide, axis=-1, keepdims=True) + 1e-06)
    normed = (stream_wide * inverse * norm_gain).astype(jnp.bfloat16)
    group = FF_WIN // w_gate.shape[0]
    group_bits = group.bit_length() - 1
    wave = devices // group
    capacity = tok_local // 4
    slot_count = capacity // group
    model_width = normed.shape[1]
    expert_ids = jnp.arange(wave, dtype=jnp.int32)
    hits = routes[:, :, None] == expert_ids[None, None, :]
    named = jnp.any(hits, axis=1)
    weight = jnp.sum(jnp.where(hits, gates[:, :, None], 0.0), axis=1)
    slot_index = jnp.cumsum(named.astype(jnp.int32), axis=0) - 1
    selector = named.T[:, None, :] & (
        slot_index.T[:, None, :] == jnp.arange(capacity)[None, :, None]
    )
    outgoing = jnp.einsum(
        "ect,td->ecd", selector.astype(jnp.bfloat16), normed, preferred_element_type=jnp.float32
    ).astype(jnp.bfloat16)
    outgoing = outgoing.reshape(devices, slot_count, model_width)
    gathered = lax.all_to_all(outgoing, "expert", split_axis=0, concat_axis=0, tiled=True)
    for bit_number in range(group_bits):
        partner = from_partner(gathered, "expert", bit_number)
        lower = my_index // 2**bit_number % 2 == 0
        gathered = jnp.where(
            lower,
            jnp.concatenate([gathered, partner], axis=1),
            jnp.concatenate([partner, gathered], axis=1),
        )
    token_rows = gathered.reshape(devices * capacity, model_width)
    dims = (((1,), (1,)), ((), ()))
    gate_pre = lax.dot_general(token_rows, w_gate, dims, preferred_element_type=jnp.float32)
    up_pre = lax.dot_general(token_rows, w_up, dims, preferred_element_type=jnp.float32)
    hidden = (jax.nn.silu(gate_pre) * up_pre).astype(jnp.bfloat16)
    piece = jnp.dot(hidden, w_down, preferred_element_type=jnp.float32).astype(jnp.bfloat16)
    piece = piece.reshape(devices, capacity, model_width)
    returned = lax.all_to_all(piece, "expert", split_axis=0, concat_axis=0, tiled=True)
    expert_out = jnp.sum(
        returned.reshape(wave, group, capacity, model_width).astype(jnp.float32), axis=1
    )
    flat_slots = expert_ids[None, :] * capacity + jnp.maximum(slot_index, 0)
    picked = jnp.take(
        expert_out.reshape(wave * capacity, model_width), flat_slots.reshape(-1), axis=0
    )
    picked = picked.reshape(tok_local, wave, model_width)
    combined = jnp.sum(weight[:, :, None] * picked, axis=1)
    return (stream_wide + combined).astype(jnp.bfloat16)


def solution(mesh):
    return jax.shard_map(
        shards,
        mesh=mesh,
        in_specs=(
            P("dp", "expert"),
            P(("dp", "expert"), None),
            P(("dp", "expert"), None),
            P("dp"),
            P(("dp", "expert"), None),
            P(),
            P(("dp", "expert"), None),
            P(("dp", "expert"), None),
            P("expert", None),
            P("expert", None),
            P("expert", None),
        ),
        out_specs=P(("dp", "expert"), None),
        check_vma=False,
    )
```

profile of v0, /device:TPU:0, one launch (start us, length us, event | category | flops | bytes accessed | tf_op | source)
XLA Modules:
  0.0 171.7 jit_solution(3322995648816507542)
XLA Ops:
  2.6 7.3 %all-to-all-start = ((bf16[32,32,128]{2,0,1:T(8,128)(2,1)}), bf16[32,32,128]{2,0,1:T(8,128)(2,1)S(1)}, u32[]{:S(2)}, u32[]{:S(2)}) async-start(bf16[32,32,128]{2,0,1:T(8,128)(2,1)} %bitcast), calls=%async_computation | async-start | bytes 524288 | tf_op jit(solution)/shard_map/all_to_all | solution.py:69
  9.9 1.2 reshape.169
  11.5 9.0 %all-to-all-done = bf16[32,32,128]{2,0,1:T(8,128)(2,1)S(1)} async-done(((bf16[32,32,128]{2,0,1:T(8,128)(2,1)}), bf16[32,32,128]{2,0,1:T(8,128)(2,1)S(1)}, u32[]{:S(2)}, u32[]{:S(2)}) %all-to-all-start) | async-done | bytes 262176 | tf_op jit(solution)/shard_map/all_to_all | solution.py:69
  20.9 4.6 %while.11 = (s32[]{:T(128)}, bf16[2,512,2,64]{1,3,2,0:T(8,128)(2,1)S(1)}, bf16[2,512,64]{1,2,0:T(8,128)(2,1)S(1)}, s32[2,512]{1,0:T(2,128)S(1)}, bf16[2,512,64]{...) while((s32[]{:T(128)}, bf16[2,512,2,64]{1,3,2,0:T(8,128)(2,1)S(1)}, ...), condition=%wide.region_3.4_spmd.clone, body=%wide.region_0.3_spmd.clone.sunk | while | flops 206899200 | bytes 1393745 | solution.py:43
  22.1 1.1 fusion.105
  24.4 1.1 fusion.105
  26.0 1.0 all_to_all.33
  27.0 2.6 %all-to-all-start.1 = ((bf16[32,32,128]{2,1,0:T(8,128)(2,1)}), bf16[32,32,128]{2,1,0:T(8,128)(2,1)S(1)}, u32[]{:S(2)}, u32[]{:S(2)}) async-start(bf16[32,32,128]{2,1,0:T(8,128)(2,1)} %all_to_all.33), calls=%async_computation.1 | async-start | bytes 524288 | tf_op jit(solution)/shard_map/all_to_all | solution.py:73
  29.8 10.3 %all-to-all-done.1 = bf16[32,32,128]{2,1,0:T(8,128)(2,1)S(1)} async-done(((bf16[32,32,128]{2,1,0:T(8,128)(2,1)}), bf16[32,32,128]{2,1,0:T(8,128)(2,1)S(1)}, u32[]{:S(2)}, u32[]{:S(2)}) %all-to-all-start.1) | async-done | bytes 262176 | tf_op jit(solution)/shard_map/all_to_all | solution.py:73
  42.2 12.7 %all_to_all.41 = bf16[32,2,2048]{2,1,0:T(2,128)(2,1)S(1)} all-to-all(bf16[32,2,2048]{2,1,0:T(2,128)(2,1)S(1)} %reshape.170), channel_id=1, replica_groups=mesh['dp'=1,'expert'=32] {'expert'}, dimensions={0} | all-to-all | bytes 524288 | tf_op jit(solution)/shard_map/all_to_all | solution.py:97
  55.2 1.9 %collective-permute-done = bf16[32,1,4096]{2,1,0:T(2,128)(2,1)S(1)} collective-permute-done((bf16[32,1,4096]{2,1,0:T(2,128)(2,1)S(1)}, bf16[32,1,4096]{2,1,0:T(2,128)(2,1)S(1)}, u32[]{:S(2)}, u32[]{:S(2)}) %collective-permute-start) | collective-permute-done | bytes 262176 | tf_op jit(solution)/shard_map/ppermute | solution.py:16
  57.1 2.3 %broadcast_select_fusion = bf16[32,2,4096]{2,1,0:T(2,128)(2,1)S(1)} fusion(pred[]{:T(512)S(6)} %eq.61, bf16[32,1,4096]{2,1,0:T(2,128)(2,1)S(1)} %collective-permute-done, bf16[32,1,4096]{2,1,0:T(2,128)(2,1)S(1)} %reshape.171), kind=kLoop, calls=%fused_computation.44 | loop fusion | flops 2359296 | bytes 1048577 | tf_op jit(solution)/shard_map/jit(_where)/select_n | solution.py:101
  60.0 13.5 %collective-permute-done.1 = bf16[32,2,4096]{2,1,0:T(2,128)(2,1)S(1)} collective-permute-done((bf16[32,2,4096]{2,1,0:T(2,128)(2,1)S(1)}, bf16[32,2,4096]{2,1,0:T(2,128)(2,1)S(1)}, u32[]{:S(2)}, u32[]{:S(2)}) %collective-permute-start.1) | collective-permute-done | bytes 524320 | tf_op jit(solution)/shard_map/ppermute | solution.py:16
  73.5 1.9 %maximum_select_fusion.1 = bf16[32,4,4096]{2,1,0:T(4,128)(2,1)S(1)} fusion(bf16[32,2,4096]{2,1,0:T(2,128)(2,1)S(1)} %collective-permute-done.1, bf16[32,2,4096]{2,1,0:T(2,128)(2,1)S(1)} %broadcast_select_fusion, pred[]{:T(512)S(6)} %eq.60), kind=kLoop, calls=%fused_computation.43 | loop fusion | flops 4718592 | bytes 2097153 | tf_op jit(solution)/shard_map/jit(_where)/select_n | solution.py:101
  75.4 1.0 collective-permute-start.2
  76.3 23.6 %collective-permute-done.2 = bf16[32,4,4096]{2,1,0:T(4,128)(2,1)} collective-permute-done((bf16[32,4,4096]{2,1,0:T(4,128)(2,1)S(1)}, bf16[32,4,4096]{2,1,0:T(4,128)(2,1)}, u32[]{:S(2)}, u32[]{:S(2)}) %collective-permute-start.2) | collective-permute-done | bytes 1048608 | tf_op jit(solution)/shard_map/ppermute | solution.py:16
  99.9 4.0 %fusion.57 = f32[256,128]{1,0:T(8,128)S(1)} fusion(bf16[128,4096]{1,0:T(8,128)(2,1)} %param.22, bf16[32,4,4096]{2,1,0:T(4,128)(2,1)} %collective-permute-done.2, bf16[32,4,4096]{2,1,0:T(4,128)(2,1)S(1)} %maximum_select_fusion.1, pred[]{:T(512)S(6)} %eq.59), kind=kOutput, calls=%fused_computation.55 | convolution fusion | flops 277872640 | bytes 3276801 | tf_op jit(solution)/shard_map/dot_general | solution.py:109
  103.9 6.2 %fusion.49 = bf16[32,8,4096]{2,1,0:T(8,128)(2,1)} fusion(bf16[128,4096]{1,0:T(8,128)(2,1)S(1)} %copy-done, f32[256,128]{1,0:T(8,128)S(1)} %fusion.57, bf16[128,4096]{1,0:T(8,128)(2,1)S(1)} %copy-done.6, bf16[32,4,4096]{2,1,0:T(4,128)(2,1)} %collective-permute-done.2, bf16[32,4,4096]{2,1,0:T(4,128)(2,1)S(1)} %maximum_select_fusion.1, pred[]{:T(512)S(6)} %eq.59), kind=kOutput, calls=%fused_computation.36 | convolution fusion | flops 547553280 | bytes 6422529 | tf_op jit(solution)/shard_map/dot_general | solution.py:111
  110.1 3.8 %all-to-all-start.3 = ((bf16[32,8,4096]{2,1,0:T(8,128)(2,1)}), bf16[32,8,4096]{2,1,0:T(8,128)(2,1)}, u32[]{:S(2)}, u32[]{:S(2)}) async-start(bf16[32,8,4096]{2,1,0:T(8,128)(2,1)} %fusion.49), calls=%async_computation.3 | async-start | bytes 4194304 | tf_op jit(solution)/shard_map/all_to_all | solution.py:113
  114.5 48.4 %all-to-all-done.3 = bf16[32,8,4096]{2,1,0:T(8,128)(2,1)} async-done(((bf16[32,8,4096]{2,1,0:T(8,128)(2,1)}), bf16[32,8,4096]{2,1,0:T(8,128)(2,1)}, u32[]{:S(2)}, u32[]{:S(2)}) %all-to-all-start.3) | async-done | bytes 2097184 | tf_op jit(solution)/shard_map/all_to_all | solution.py:113
  162.9 2.0 %convert_reduce_fusion = f32[4,8,4096]{2,1,0:T(8,128)S(1)} fusion(bf16[32,8,4096]{2,1,0:T(8,128)(2,1)} %all-to-all-done.3), kind=kLoop, calls=%fused_computation.39 | loop fusion | flops 1966080 | bytes 2621440 | tf_op jit(solution)/shard_map/reduce_sum | solution.py:114
  164.8 2.6 %gather_fusion = f32[128,4096]{1,0:T(8,128)} fusion(f32[32,4096]{1,0:T(8,128)S(1)} %bitcast.111, s32[1024]{0:T(1024)S(1)} %pad_clamp_fusion), kind=kCustom, calls=%fused_computation | custom fusion | bytes 4194816 | tf_op jit(solution)/shard_map/jit(_take)/gather | solution.py:118
  167.4 1.9 %gather.7 = f32[32,4,4096]{2,1,0:T(4,128)S(1)} reshape(f32[128,4096]{1,0:T(8,128)} %gather_fusion) | data formatting | bytes 4194304 | tf_op jit(solution)/shard_map/jit(_take)/gather | solution.py:118
  169.3 1.7 multiply_reduce_fusion
  (57 shorter events, 10.4 us)
Async XLA Ops:
  0.0 103.9 %copy-start = (bf16[128,4096]{1,0:T(8,128)(2,1)S(1)}, bf16[128,4096]{1,0:T(8,128)(2,1)}, u32[]{:S(2)}) copy-start(bf16[128,4096]{1,0:T(8,128)(2,1)} %param.23) | copy-start | bytes 3145732
  0.0 11.5 %copy-start.4 = (s32[1024]{0:T(1024)S(1)}, s32[1024]{0:T(1024)}, u32[]{:S(2)}) copy-start(s32[1024]{0:T(1024)} %param.16) | copy-start | bytes 12292
  2.6 17.9 %all-to-all-start = ((bf16[32,32,128]{2,0,1:T(8,128)(2,1)}), bf16[32,32,128]{2,0,1:T(8,128)(2,1)S(1)}, u32[]{:S(2)}, u32[]{:S(2)}) async-start(bf16[32,32,128]{2,0,1:T(8,128)(2,1)} %bitcast), calls=%async_computation | async-start | bytes 524288 | tf_op jit(solution)/shard_map/all_to_all | solution.py:69
  25.5 4.0 %copy-start.3 = (s32[32,8]{0,1:T(8,128)S(1)}, s32[32,8]{0,1:T(8,128)}, u32[]{:S(2)}) copy-start(s32[32,8]{0,1:T(8,128)} %param.19) | copy-start | bytes 3076
  25.6 14.6 %copy-start.1 = (bf16[32,4096]{1,0:T(8,128)(2,1)S(1)}, bf16[32,4096]{1,0:T(8,128)(2,1)}, u32[]{:S(2)}) copy-start(bf16[32,4096]{1,0:T(8,128)(2,1)} %param.17) | copy-start | bytes 786436
  25.6 14.8 %copy-start.2 = (f32[4096]{0:T(1024)S(1)}, f32[4096]{0:T(1024)}, u32[]{:S(2)}) copy-start(f32[4096]{0:T(1024)} %param.18) | copy-start | bytes 49156
  27.0 13.2 %all-to-all-start.1 = ((bf16[32,32,128]{2,1,0:T(8,128)(2,1)}), bf16[32,32,128]{2,1,0:T(8,128)(2,1)S(1)}, u32[]{:S(2)}, u32[]{:S(2)}) async-start(bf16[32,32,128]{2,1,0:T(8,128)(2,1)} %all_to_all.33), calls=%async_computation.1 | async-start | bytes 524288 | tf_op jit(solution)/shard_map/all_to_all | solution.py:73
  55.1 2.0 %collective-permute-start = (bf16[32,1,4096]{2,1,0:T(2,128)(2,1)S(1)}, bf16[32,1,4096]{2,1,0:T(2,128)(2,1)S(1)}, u32[]{:S(2)}, u32[]{:S(2)}) collective-permute-start(bf16[32,1,4096]{2,1,0:T(2,128)(2,1)S(1)} %reshape.171), channel_id=1, source_target_pairs={{0,1},{1,0},{2,3},{3,2},{4,5},{5,4},{6,7},{7,6},{8,9},{9,8},{10,11... | collective-permute-start | bytes 786440 | tf_op jit(solution)/shard_map/ppermute | solution.py:16
  59.5 14.0 %collective-permute-start.1 = (bf16[32,2,4096]{2,1,0:T(2,128)(2,1)S(1)}, bf16[32,2,4096]{2,1,0:T(2,128)(2,1)S(1)}, u32[]{:S(2)}, u32[]{:S(2)}) collective-permute-start(bf16[32,2,4096]{2,1,0:T(2,128)(2,1)S(1)} %broadcast_select_fusion), channel_id=1, source_target_pairs={{0,2},{1,3},{2,0},{3,1},{4,6},{5,7},{6,4},{7,5},{8,10},{9,11},{10,... | collective-permute-start | bytes 1572872 | tf_op jit(solution)/shard_map/ppermute | solution.py:16
  75.4 24.5 %collective-permute-start.2 = (bf16[32,4,4096]{2,1,0:T(4,128)(2,1)S(1)}, bf16[32,4,4096]{2,1,0:T(4,128)(2,1)}, u32[]{:S(2)}, u32[]{:S(2)}) collective-permute-start(bf16[32,4,4096]{2,1,0:T(4,128)(2,1)S(1)} %maximum_select_fusion.1), channel_id=1, source_target_pairs={{0,4},{1,5},{2,6},{3,7},{4,0},{5,1},{6,2},{7,3},{8,12},{9,13},{10,... | collective-permute-start | bytes 3145736 | tf_op jit(solution)/shard_map/ppermute | solution.py:16
  76.3 27.6 %copy-start.6 = (bf16[128,4096]{1,0:T(8,128)(2,1)S(1)}, bf16[128,4096]{1,0:T(8,128)(2,1)}, u32[]{:S(2)}) copy-start(bf16[128,4096]{1,0:T(8,128)(2,1)} %param.21) | copy-start | bytes 3145732
  110.1 4.2 %copy-start.5 = (f32[32,8]{0,1:T(8,128)S(1)}, f32[32,8]{0,1:T(8,128)}, u32[]{:S(2)}) copy-start(f32[32,8]{0,1:T(8,128)} %param.20) | copy-start | bytes 3076
  110.1 52.7 %all-to-all-start.3 = ((bf16[32,8,4096]{2,1,0:T(8,128)(2,1)}), bf16[32,8,4096]{2,1,0:T(8,128)(2,1)}, u32[]{:S(2)}, u32[]{:S(2)}) async-start(bf16[32,8,4096]{2,1,0:T(8,128)(2,1)} %fusion.49), calls=%async_computation.3 | async-start | bytes 4194304 | tf_op jit(solution)/shard_map/all_to_all | solution.py:113
where the time goes:
time: 172 us
  waiting for transfers between devices  107 us (62%)
  starting transfers between devices  15.3 us (9%)
  matrix products  14.6 us (8%)
  blocking collectives  12.7 us (7%)
  local copies, waits for them, and re-layouts  11.8 us (7%)
  other arithmetic  10.4 us (6%)
    all_to_all x1, waiting for transfers between devices, shards(): lax.all_to_all(piece, 'expert', split_axis=0, concat_axis=0, tiled=True)  48.4 us
    ppermute x3, waiting for transfers between devices, from_partner(): return lax.ppermute(value, axis, pairs)  39 us
    all_to_all x1, blocking collectives, shards(): lax.all_to_all(outgoing, 'expert', split_axis=0, concat_axis=0, tiled=True)  12.7 us
    all_to_all x1, waiting for transfers between devices, shards(): lax.all_to_all(attended_heads, 'expert', split_axis=0, concat_axis=1, til...  10.3 us
    all_to_all x1, waiting for transfers between devices, shards(): lax.all_to_all(spread, 'expert', split_axis=1, concat_axis=0, tiled=True)  8.96 us
    all_to_all x1, starting transfers between devices, shards(): lax.all_to_all(spread, 'expert', split_axis=1, concat_axis=0, tiled=True)  7.3 us
    dot_general x1, matrix products, shards(): jnp.dot(hidden, w_down, preferred_element_type=jnp.float32)  6.19 us
    gather x2, local copies, waits for them, and re-layouts, shards(): jnp.take(expert_out.reshape(wave * capacity, model_width), flat_slots.res...  4.43 us
  transfers between devices with their start and end apart: 6, of which 6 were waited for; matrix products, arithmetic and copies ran while one was open for 1% of the time, Pallas kernels for 0%

commit v1 on v0

--- a/solution.py
+++ b/solution.py
@@ -70,7 +70,12 @@
     key_mine = arrived_heads[:, 0, :HEAD_DIM]
     value_mine = arrived_heads[:, 0, HEAD_DIM:]
     attended_heads = attend(queries, key_mine, value_mine, span_ids)
-    attended = lax.all_to_all(attended_heads, "expert", split_axis=0, concat_axis=1, tiled=True)
+    attended = jnp.concatenate(
+        lax.all_to_all(
+            jnp.stack(jnp.split(attended_heads, lax.axis_size("expert"), axis=0)), "expert", 0, 0
+        ),
+        axis=1,
+    )
     stream_wide = residual.astype(jnp.float32) + attended.astype(jnp.float32)
     stream = stream_wide.astype(jnp.bfloat16)
     stream_wide = stream.astype(jnp.float32)

time: 172 us -> 194 us (1.13)
  local copies, waits for them, and re-layouts: 11.8 us -> 33.2 us
    unnamed x19 -> x49, local copies, waits for them, and re-layouts: 1.13 us -> 19.8 us
    another operation x0 -> x33, local copies, waits for them, and re-layouts: none -> 3.51 us  [shards(): jnp.stack(jnp.split(attended_heads, lax.axis_size('expert'), axis=0))]
where the time goes in v1:
time: 194 us; the launch traced here: 193 us
  waiting for transfers between devices  107 us (55%)
  local copies, waits for them, and re-layouts  33.2 us (17%)
  starting transfers between devices  15.3 us (8%)
  matrix products  14.8 us (8%)
  blocking collectives  12.7 us (7%)
  other arithmetic  10.3 us (5%)
    all_to_all x1, waiting for transfers between devices, shards(): lax.all_to_all(piece, 'expert', split_axis=0, concat_axis=0, tiled=True)  48.4 us
    ppermute x3, waiting for transfers between devices, from_partner(): return lax.ppermute(value, axis, pairs)  39 us
    unnamed x49, local copies, waits for them, and re-layouts  19.8 us
    all_to_all x1, blocking collectives, shards(): lax.all_to_all(outgoing, 'expert', split_axis=0, concat_axis=0, tiled=True)  12.7 us
    all_to_all x1, waiting for transfers between devices, shards(): lax.all_to_all(jnp.stack(jnp.split(attended_heads, lax.axis_size('expert'...  10.3 us
    all_to_all x1, waiting for transfers between devices, shards(): lax.all_to_all(spread, 'expert', split_axis=1, concat_axis=0, tiled=True)  8.97 us
    all_to_all x1, starting transfers between devices, shards(): lax.all_to_all(spread, 'expert', split_axis=1, concat_axis=0, tiled=True)  7.3 us
    dot_general x1, matrix products, shards(): jnp.dot(hidden, w_down, preferred_element_type=jnp.float32)  6.5 us
  transfers between devices with their start and end apart: 6, of which 6 were waited for; matrix products, arithmetic and copies ran while one was open for 1% of the time, Pallas kernels for 0%

profile of v1, /device:TPU:0, one launch (start us, length us, event | category | flops | bytes accessed | tf_op | source)
XLA Modules:
  0.0 193.3 jit_solution(11634511843339990276)
XLA Ops:
  2.6 7.3 %all-to-all-start = ((bf16[32,32,128]{2,0,1:T(8,128)(2,1)}), bf16[32,32,128]{2,0,1:T(8,128)(2,1)S(1)}, u32[]{:S(2)}, u32[]{:S(2)}) async-start(bf16[32,32,128]{2,0,1:T(8,128)(2,1)} %bitcast), calls=%async_computation | async-start | bytes 524288 | tf_op jit(solution)/shard_map/all_to_all | solution.py:69
  9.9 1.2 reshape.170
  11.5 9.0 %all-to-all-done = bf16[32,32,128]{2,0,1:T(8,128)(2,1)S(1)} async-done(((bf16[32,32,128]{2,0,1:T(8,128)(2,1)}), bf16[32,32,128]{2,0,1:T(8,128)(2,1)S(1)}, u32[]{:S(2)}, u32[]{:S(2)}) %all-to-all-start) | async-done | bytes 262176 | tf_op jit(solution)/shard_map/all_to_all | solution.py:69
  20.9 4.6 %while.11 = (s32[]{:T(128)}, bf16[2,512,2,64]{1,3,2,0:T(8,128)(2,1)S(1)}, bf16[2,512,64]{1,2,0:T(8,128)(2,1)S(1)}, s32[2,512]{1,0:T(2,128)S(1)}, bf16[2,512,64]{...) while((s32[]{:T(128)}, bf16[2,512,2,64]{1,3,2,0:T(8,128)(2,1)S(1)}, ...), condition=%wide.region_3.4_spmd.clone, body=%wide.region_0.3_spmd.clone.sunk | while | flops 206899200 | bytes 1393745 | solution.py:43
  21.1 0.9 fusion.105
  22.1 1.1 fusion.106
  24.4 1.1 fusion.106
  48.3 2.6 %all-to-all-start.1 = ((bf16[32,32,128]{2,1,0:T(8,128)(2,1)}), bf16[32,32,128]{2,1,0:T(8,128)(2,1)S(1)}, u32[]{:S(2)}, u32[]{:S(2)}) async-start(bf16[32,32,128]{2,1,0:T(8,128)(2,1)} %constant_dynamic-update-slice_fusion), calls=%async_computation.1 | async-start | bytes 524288 | tf_op jit(solution)/shard_map/all_to_all | solution.py:74
  51.2 10.3 %all-to-all-done.1 = bf16[32,32,128]{2,1,0:T(8,128)(2,1)S(1)} async-done(((bf16[32,32,128]{2,1,0:T(8,128)(2,1)}), bf16[32,32,128]{2,1,0:T(8,128)(2,1)S(1)}, u32[]{:S(2)}, u32[]{:S(2)}) %all-to-all-start.1) | async-done | bytes 262176 | tf_op jit(solution)/shard_map/all_to_all | solution.py:74
  63.5 12.7 %all_to_all.33 = bf16[32,2,2048]{2,1,0:T(2,128)(2,1)S(1)} all-to-all(bf16[32,2,2048]{2,1,0:T(2,128)(2,1)S(1)} %reshape.171), channel_id=1, replica_groups=mesh['dp'=1,'expert'=32] {'expert'}, dimensions={0} | all-to-all | bytes 524288 | tf_op jit(solution)/shard_map/all_to_all | solution.py:102
  76.6 1.9 collective-permute-done
  78.5 2.3 %broadcast_select_fusion = bf16[32,2,4096]{2,1,0:T(2,128)(2,1)S(1)} fusion(pred[]{:T(512)S(6)} %eq.61, bf16[32,1,4096]{2,1,0:T(2,128)(2,1)S(1)} %collective-permute-done, bf16[32,1,4096]{2,1,0:T(2,128)(2,1)S(1)} %reshape.172), kind=kLoop, calls=%fused_computation.44 | loop fusion | flops 2359296 | bytes 1048577 | tf_op jit(solution)/shard_map/jit(_where)/select_n | solution.py:106
  81.4 13.5 %collective-permute-done.1 = bf16[32,2,4096]{2,1,0:T(2,128)(2,1)S(1)} collective-permute-done((bf16[32,2,4096]{2,1,0:T(2,128)(2,1)S(1)}, bf16[32,2,4096]{2,1,0:T(2,128)(2,1)S(1)}, u32[]{:S(2)}, u32[]{:S(2)}) %collective-permute-start.1) | collective-permute-done | bytes 524320 | tf_op jit(solution)/shard_map/ppermute | solution.py:16
  94.9 1.9 maximum_select_fusion.1
  96.8 1.0 collective-permute-start.2
  97.7 23.6 %collective-permute-done.2 = bf16[32,4,4096]{2,1,0:T(4,128)(2,1)} collective-permute-done((bf16[32,4,4096]{2,1,0:T(4,128)(2,1)S(1)}, bf16[32,4,4096]{2,1,0:T(4,128)(2,1)}, u32[]{:S(2)}, u32[]{:S(2)}) %collective-permute-start.2) | collective-permute-done | bytes 1048608 | tf_op jit(solution)/shard_map/ppermute | solution.py:16
  121.3 4.0 %fusion.57 = f32[256,128]{1,0:T(8,128)S(1)} fusion(bf16[128,4096]{1,0:T(8,128)(2,1)} %param.22, bf16[32,4,4096]{2,1,0:T(4,128)(2,1)} %collective-permute-done.2, bf16[32,4,4096]{2,1,0:T(4,128)(2,1)S(1)} %maximum_select_fusion.1, pred[]{:T(512)S(6)} %eq.59), kind=kOutput, calls=%fused_computation.55 | convolution fusion | flops 277872640 | bytes 3276801 | tf_op jit(solution)/shard_map/dot_general | solution.py:114
  125.3 6.5 %fusion.49 = bf16[32,8,4096]{2,1,0:T(8,128)(2,1)} fusion(bf16[128,4096]{1,0:T(8,128)(2,1)S(1)} %copy-done, f32[256,128]{1,0:T(8,128)S(1)} %fusion.57, bf16[128,4096]{1,0:T(8,128)(2,1)} %param.21, bf16[32,4,4096]{2,1,0:T(4,128)(2,1)} %collective-permute-done.2, bf16[32,4,4096]{2,1,0:T(4,128)(2,1)S(1)} %maximum_select_fusion.1, pred[]{:T(512)S(6)} %eq.59), kind=kOutput, calls=%fused_computation.36 | convolution fusion | flops 547553280 | bytes 6422529 | tf_op jit(solution)/shard_map/dot_general | solution.py:116
  131.8 3.8 %all-to-all-start.3 = ((bf16[32,8,4096]{2,1,0:T(8,128)(2,1)}), bf16[32,8,4096]{2,1,0:T(8,128)(2,1)}, u32[]{:S(2)}, u32[]{:S(2)}) async-start(bf16[32,8,4096]{2,1,0:T(8,128)(2,1)} %fusion.49), calls=%async_computation.3 | async-start | bytes 4194304 | tf_op jit(solution)/shard_map/all_to_all | solution.py:118
  136.2 48.4 %all-to-all-done.3 = bf16[32,8,4096]{2,1,0:T(8,128)(2,1)} async-done(((bf16[32,8,4096]{2,1,0:T(8,128)(2,1)}), bf16[32,8,4096]{2,1,0:T(8,128)(2,1)}, u32[]{:S(2)}, u32[]{:S(2)}) %all-to-all-start.3) | async-done | bytes 2097184 | tf_op jit(solution)/shard_map/all_to_all | solution.py:118
  184.5 1.9 %convert_reduce_fusion = f32[4,8,4096]{2,1,0:T(8,128)S(1)} fusion(bf16[32,8,4096]{2,1,0:T(8,128)(2,1)} %all-to-all-done.3), kind=kLoop, calls=%fused_computation.39 | loop fusion | flops 1966080 | bytes 2621440 | tf_op jit(solution)/shard_map/reduce_sum | solution.py:119
  186.5 2.6 %gather_fusion = f32[128,4096]{1,0:T(8,128)} fusion(f32[32,4096]{1,0:T(8,128)S(1)} %bitcast.180, s32[1024]{0:T(1024)S(1)} %pad_clamp_fusion), kind=kCustom, calls=%fused_computation | custom fusion | bytes 4194816 | tf_op jit(solution)/shard_map/jit(_take)/gather | solution.py:123
  189.1 1.9 gather.7
  190.9 1.7 multiply_reduce_fusion
  (121 shorter events, 31.8 us)
Async XLA Ops:
  0.0 125.3 %copy-start = (bf16[128,4096]{1,0:T(8,128)(2,1)S(1)}, bf16[128,4096]{1,0:T(8,128)(2,1)}, u32[]{:S(2)}) copy-start(bf16[128,4096]{1,0:T(8,128)(2,1)} %param.23) | copy-start | bytes 3145732
  0.0 11.5 %copy-start.4 = (s32[1024]{0:T(1024)S(1)}, s32[1024]{0:T(1024)}, u32[]{:S(2)}) copy-start(s32[1024]{0:T(1024)} %param.16) | copy-start | bytes 12292
  2.6 17.9 %all-to-all-start = ((bf16[32,32,128]{2,0,1:T(8,128)(2,1)}), bf16[32,32,128]{2,0,1:T(8,128)(2,1)S(1)}, u32[]{:S(2)}, u32[]{:S(2)}) async-start(bf16[32,32,128]{2,0,1:T(8,128)(2,1)} %bitcast), calls=%async_computation | async-start | bytes 524288 | tf_op jit(solution)/shard_map/all_to_all | solution.py:69
  25.8 25.1 %copy-start.3 = (s32[32,8]{0,1:T(8,128)S(1)}, s32[32,8]{0,1:T(8,128)}, u32[]{:S(2)}) copy-start(s32[32,8]{0,1:T(8,128)} %param.19) | copy-start | bytes 3076
  25.8 35.7 %copy-start.1 = (bf16[32,4096]{1,0:T(8,128)(2,1)S(1)}, bf16[32,4096]{1,0:T(8,128)(2,1)}, u32[]{:S(2)}) copy-start(bf16[32,4096]{1,0:T(8,128)(2,1)} %param.17) | copy-start | bytes 786436
  26.0 35.7 %copy-start.2 = (f32[4096]{0:T(1024)S(1)}, f32[4096]{0:T(1024)}, u32[]{:S(2)}) copy-start(f32[4096]{0:T(1024)} %param.18) | copy-start | bytes 49156
  48.3 13.2 %all-to-all-start.1 = ((bf16[32,32,128]{2,1,0:T(8,128)(2,1)}), bf16[32,32,128]{2,1,0:T(8,128)(2,1)S(1)}, u32[]{:S(2)}, u32[]{:S(2)}) async-start(bf16[32,32,128]{2,1,0:T(8,128)(2,1)} %constant_dynamic-update-slice_fusion), calls=%async_computation.1 | async-start | bytes 524288 | tf_op jit(solution)/shard_map/all_to_all | solution.py:74
  76.5 2.0 %collective-permute-start = (bf16[32,1,4096]{2,1,0:T(2,128)(2,1)S(1)}, bf16[32,1,4096]{2,1,0:T(2,128)(2,1)S(1)}, u32[]{:S(2)}, u32[]{:S(2)}) collective-permute-start(bf16[32,1,4096]{2,1,0:T(2,128)(2,1)S(1)} %reshape.172), channel_id=1, source_target_pairs={{0,1},{1,0},{2,3},{3,2},{4,5},{5,4},{6,7},{7,6},{8,9},{9,8},{10,11... | collective-permute-start | bytes 786440 | tf_op jit(solution)/shard_map/ppermute | solution.py:16
  80.8 14.0 %collective-permute-start.1 = (bf16[32,2,4096]{2,1,0:T(2,128)(2,1)S(1)}, bf16[32,2,4096]{2,1,0:T(2,128)(2,1)S(1)}, u32[]{:S(2)}, u32[]{:S(2)}) collective-permute-start(bf16[32,2,4096]{2,1,0:T(2,128)(2,1)S(1)} %broadcast_select_fusion), channel_id=1, source_target_pairs={{0,2},{1,3},{2,0},{3,1},{4,6},{5,7},{6,4},{7,5},{8,10},{9,11},{10,... | collective-permute-start | bytes 1572872 | tf_op jit(solution)/shard_map/ppermute | solution.py:16
  96.8 24.5 %collective-permute-start.2 = (bf16[32,4,4096]{2,1,0:T(4,128)(2,1)S(1)}, bf16[32,4,4096]{2,1,0:T(4,128)(2,1)}, u32[]{:S(2)}, u32[]{:S(2)}) collective-permute-start(bf16[32,4,4096]{2,1,0:T(4,128)(2,1)S(1)} %maximum_select_fusion.1), channel_id=1, source_target_pairs={{0,4},{1,5},{2,6},{3,7},{4,0},{5,1},{6,2},{7,3},{8,12},{9,13},{10,... | collective-permute-start | bytes 3145736 | tf_op jit(solution)/shard_map/ppermute | solution.py:16
  131.8 4.2 %copy-start.5 = (f32[32,8]{0,1:T(8,128)S(1)}, f32[32,8]{0,1:T(8,128)}, u32[]{:S(2)}) copy-start(f32[32,8]{0,1:T(8,128)} %param.20) | copy-start | bytes 3076
  131.8 52.7 %all-to-all-start.3 = ((bf16[32,8,4096]{2,1,0:T(8,128)(2,1)}), bf16[32,8,4096]{2,1,0:T(8,128)(2,1)}, u32[]{:S(2)}, u32[]{:S(2)}) async-start(bf16[32,8,4096]{2,1,0:T(8,128)(2,1)} %fusion.49), calls=%async_computation.3 | async-start | bytes 4194304 | tf_op jit(solution)/shard_map/all_to_all | solution.py:118
